TPU v7x, 32 devices: a whole 2x2x4 slice. The times are simulated.
32 devices in a mesh: pb: 4 (over y, core), kv: 8 (over z, x).
Axes of the slice: x: 2, y: 2, z: 4, core: 2. Of those that a mesh axis runs over, the one named last changes fastest.
Arguments:
- queries: bfloat16 [8192, 4096], P(('pb', 'kv')), may hold values from -6 to 6
- keys: bfloat16 [1024, 4096], P(('pb', 'kv')), may hold values from -6 to 6
- values: bfloat16 [1024, 4096], P(('pb', 'kv')), may hold values from -6 to 6
- key_lists: int32 [64, 8], P('pb'), may hold values from 0 to 7, as said below
- counts: int32 [64], P('pb'), may hold values from 1 to 8, as said below
Outputs:
- attended: bfloat16 [8192, 4096], P(('pb', 'kv'))
Inputs may be any that keep to these rules, and one draw needn't show every extreme that they name: For every query block the first counts entries of its row of key_lists name different key blocks; entries past counts are valid block numbers that do not take part. `counts`: some query block uses all 8 entries of its list.
All inputs are finite; a program needn't handle non-finite values.
Results may differ from a plain program's by a relative error of at most 0.011.
Values may be sent and summed in bfloat16 or wider, within the bound.
A program may use at most 64 MiB of HBM per device.

v0:
```python
import math

import jax
import jax.numpy as jnp
from jax import lax
from jax.sharding import PartitionSpec as P

HEADS = 32
HD = 128
BLK = 128
MOST = 8


def regroup(split_array, kv_count, pb_count):
    tokens_each = split_array.shape[0] // (kv_count * pb_count)
    shaped = split_array.reshape(kv_count, pb_count, tokens_each, split_array.shape[1])
    return shaped.transpose(1, 0, 2, 3).reshape(-1, split_array.shape[1])


def per_device(queries, keys, values, key_lists, counts):
    kv_count = lax.axis_size("kv")
    pb_count = lax.axis_size("pb")
    head_local = HEADS // kv_count
    scaling = HD ** (-0.5)
    key_whole, value_whole = (
        lax.all_gather(keys, "pb", axis=0, tiled=True),
        lax.all_gather(values, "pb", axis=0, tiled=True),
    )
    key_split, value_split = (
        lax.all_to_all(key_whole, "kv", split_axis=1, concat_axis=0, tiled=True),
        lax.all_to_all(value_whole, "kv", split_axis=1, concat_axis=0, tiled=True),
    )
    key_heads = regroup(key_split, kv_count, pb_count)
    value_heads = regroup(value_split, kv_count, pb_count)
    key_blocks = key_heads.reshape(-1, BLK, head_local, HD)
    value_blocks = value_heads.reshape(-1, BLK, head_local, HD)
    slot_of_key = jnp.arange(MOST * BLK, dtype=jnp.int32) // BLK

    def padded_group(item):
        group_queries, group_lists, group_counts = item
        members = group_queries.shape[0]
        listed_keys = key_blocks[group_lists].reshape(members, MOST * BLK, head_local, HD)
        listed_values = value_blocks[group_lists].reshape(members, MOST * BLK, head_local, HD)
        scores = (
            jnp.einsum(
                "gqhd,gkhd->ghqk", group_queries, listed_keys, preferred_element_type=jnp.float32
            )
            * scaling
        )
        usable = (slot_of_key[None, :] < group_counts[:, None])[:, None, None, :]
        largest = jnp.max(jnp.where(usable, scores, -jnp.inf), axis=-1, keepdims=True)
        raised = jnp.where(usable, jnp.exp(scores - largest), 0.0)
        totals = jnp.sum(raised, axis=-1, keepdims=True)
        weights = (raised / totals).astype(jnp.bfloat16)
        output = jnp.einsum(
            "ghqk,gkhd->gqhd", weights, listed_values, preferred_element_type=jnp.float32
        )
        return output.astype(jnp.bfloat16)

    query_blocks = queries.reshape(-1, BLK, queries.shape[1])
    exchanged = lax.all_to_all(query_blocks, "kv", split_axis=2, concat_axis=0, tiled=True)
    block_total = exchanged.shape[0]
    rows = exchanged.shape[1]
    per_group = math.gcd(block_total, max(1, 512 // rows))
    group_total = block_total // per_group
    grouped = exchanged.reshape(group_total, per_group, rows, head_local, HD)
    lists_grouped = key_lists.reshape(group_total, per_group, key_lists.shape[1])
    counts_grouped = counts.reshape(group_total, per_group)
    produced = lax.map(padded_group, (grouped, lists_grouped, counts_grouped))
    joined = produced.reshape(block_total, rows, head_local * HD)
    result = lax.all_to_all(joined, "kv", split_axis=0, concat_axis=2, tiled=True)
    return result.reshape(queries.shape)


def solution(mesh):
    return jax.shard_map(
        per_device,
        mesh=mesh,
        in_specs=(
            P(("pb", "kv"), None),
            P(("pb", "kv"), None),
            P(("pb", "kv"), None),
            P("pb", None),
            P("pb"),
        ),
        out_specs=P(("pb", "kv"), None),
        check_vma=False,
    )
```

profile of v0, /device:TPU:0, one launch (start us, length us, event | category | flops | bytes accessed | tf_op | source)
XLA Modules:
  0.0 322.0 jit_solution(6022198626749850867)
XLA Ops:
  6.5 0.7 all-gather.3.cloned.1.call-update
  7.3 21.1 %all-gather.3.cloned.1.call-done = bf16[128,4096]{1,0:T(8,128)(2,1)} async-done(((bf16[32,4096]{1,0:T(8,128)(2,1)}), bf16[128,4096]{1,0:T(8,128)(2,1)}) %all-gather.3.cloned.1.call-update) | async-done | bytes 1048592 | tf_op jit(solution)/shard_map/all_gather | solution.py:27
  28.4 2.3 copy.44
  30.6 5.5 %all-to-all-start = ((bf16[128,8,512]{0,2,1:T(8,128)(2,1)}), bf16[128,8,512]{0,2,1:T(8,128)(2,1)S(1)}, u32[]{:S(2)}, u32[]{:S(2)}) async-start(bf16[128,8,512]{0,2,1:T(8,128)(2,1)} %bitcast.1), calls=%async_computation | async-start | bytes 2097152 | tf_op jit(solution)/shard_map/all_to_all | solution.py:31
  36.2 0.7 all-gather.5.cloned.1.call-update
  36.9 18.9 %all-gather.5.cloned.1.call-done = bf16[128,4096]{1,0:T(8,128)(2,1)} async-done(((bf16[32,4096]{1,0:T(8,128)(2,1)}), bf16[128,4096]{1,0:T(8,128)(2,1)}) %all-gather.5.cloned.1.call-update) | async-done | bytes 1048592 | tf_op jit(solution)/shard_map/all_gather | solution.py:26
  55.8 2.3 copy.50
  58.0 4.3 %all-to-all-done = bf16[128,8,512]{0,2,1:T(8,128)(2,1)S(1)} async-done(((bf16[128,8,512]{0,2,1:T(8,128)(2,1)}), bf16[128,8,512]{0,2,1:T(8,128)(2,1)S(1)}, u32[]{:S(2)}, u32[]{:S(2)}) %all-to-all-start) | async-done | bytes 1048608 | tf_op jit(solution)/shard_map/all_to_all | solution.py:31
  62.3 3.6 %all-to-all-start.2 = ((bf16[128,8,512]{0,2,1:T(8,128)(2,1)}), bf16[128,8,512]{0,2,1:T(8,128)(2,1)S(1)}, u32[]{:S(2)}, u32[]{:S(2)}) async-start(bf16[128,8,512]{0,2,1:T(8,128)(2,1)} %bitcast.9), calls=%async_computation.2 | async-start | bytes 2097152 | tf_op jit(solution)/shard_map/all_to_all | solution.py:30
  66.0 6.2 %copy.47 = bf16[2,128,4096]{1,0,2:T(2,128)(2,1)} copy(bf16[2,128,4096]{2,1,0:T(8,128)(2,1)} %bitcast.67) | data formatting | bytes 4194304 | tf_op jit(solution)/shard_map/reshape | solution.py:60
  72.2 19.7 %all-to-all-done.2 = bf16[128,8,512]{0,2,1:T(8,128)(2,1)S(1)} async-done(((bf16[128,8,512]{0,2,1:T(8,128)(2,1)}), bf16[128,8,512]{0,2,1:T(8,128)(2,1)S(1)}, u32[]{:S(2)}, u32[]{:S(2)}) %all-to-all-start.2) | async-done | bytes 1048608 | tf_op jit(solution)/shard_map/all_to_all | solution.py:30
  91.9 4.3 %all-to-all-start.1 = ((bf16[2,128,4096]{1,0,2:T(2,128)(2,1)}), bf16[2,128,4096]{1,0,2:T(2,128)(2,1)}, u32[]{:S(2)}, u32[]{:S(2)}) async-start(bf16[2,128,4096]{1,0,2:T(2,128)(2,1)} %copy.47), calls=%async_computation.1 | async-start | bytes 4194304 | tf_op jit(solution)/shard_map/all_to_all | solution.py:61
  96.4 0.5 copy.45
  97.0 1.0 copy.46
  98.0 1.3 reshape_reshape.6
  99.3 0.5 copy.51
  99.9 1.0 copy.52
  100.9 1.3 reshape_reshape.7
  102.3 41.8 %all-to-all-done.1 = bf16[2,128,4096]{1,0,2:T(2,128)(2,1)} async-done(((bf16[2,128,4096]{1,0,2:T(2,128)(2,1)}), bf16[2,128,4096]{1,0,2:T(2,128)(2,1)}, u32[]{:S(2)}, u32[]{:S(2)}) %all-to-all-start.1) | async-done | bytes 2097184 | tf_op jit(solution)/shard_map/all_to_all | solution.py:61
  144.1 1.9 copy.48
  145.9 1.5 copy.49
  147.4 109.7 %while.11 = (s32[]{:T(128)}, bf16[4,4,128,4,128]{2,4,3,1,0:T(8,128)(2,1)}, s32[4,4,8]{2,1,0:T(4,128)S(1)}, bf16[8,128,4,128]{3,2,1,0:T(4,128)(2,1)S(1)}, s32[4,4...) while((s32[]{:T(128)}, ...), condition=%wide.region_3.4_spmd.clone, body=%wide.region_0.3_spmd.clone.sunk | while | flops 1090795648 | bytes 59807756 | solution.py:69
  147.4 0.1 reshape.141
  147.5 5.7 %gather_fusion = bf16[32,128,4,128]{3,2,1,0:T(4,128)(2,1)} fusion(bf16[8,128,4,128]{3,2,1,0:T(4,128)(2,1)S(1)} %get-tuple-element.177, s32[1024]{0:T(1024)S(1)} %pad_clamp_fusion.2), kind=kCustom, calls=%fused_computation.1.clone.clone.1 | custom fusion | bytes 8388736 | tf_op jit(solution)/shard_map/while/body/eval_jaxpr/gather | solution.py:42
  153.3 3.7 %fusion.43 = f32[4,4,128,1024]{3,2,1,0:T(8,128)S(1)} fusion(bf16[4,1024,4,128]{3,2,1,0:T(4,128)(2,1)} %bitcast.57, bf16[4,4,128,4,128]{2,4,3,1,0:T(8,128)(2,1)} %get-tuple-element.176, s32[]{:T(128)} %get-tuple-element.163), kind=kOutput, calls=%fused_computation.11.clone.1 | convolution fusion | flops 536870912 | bytes 13107712 | tf_op jit(solution)/shard_map/while/body/eval_jaxpr/gqhd,gkhd->ghqk/dot_general | solution.py:45
  157.0 4.7 %fusion.45 = (f32[4,4,128]{2,1,0:T(4,128)S(1)}, f32[4,4,128,1024]{3,2,1,0:T(8,128)}) fusion(f32[4,4,128,1024]{3,2,1,0:T(8,128)S(1)} %fusion.43, pred[4,1024]{1,0:T(4,128)(4,1)S(1)} %broadcast_compare_fusion.2), kind=kOutput, calls=%fused_computation.36.clone.1 | output fusion | flops 12583935 | bytes 16789504 | tf_op jit(solution)/shard_map/while/body/eval_jaxpr/sub | solution.py:52
  161.8 5.8 %gather_fusion.1 = bf16[32,128,4,128]{3,2,1,0:T(4,128)(2,1)} fusion(bf16[8,128,4,128]{3,2,1,0:T(4,128)(2,1)S(1)} %get-tuple-element.174, s32[1024]{0:T(1024)S(1)} %pad_clamp_fusion.2), kind=kCustom, calls=%fused_computation.clone.clone.1 | custom fusion | bytes 8388736 | tf_op jit(solution)/shard_map/while/body/eval_jaxpr/gather | solution.py:43
  167.5 7.3 %fusion.46 = bf16[4,4,128,4,128]{2,4,3,1,0:T(8,128)(2,1)} fusion(bf16[4,4,128,4,128]{2,4,3,1,0:T(8,128)(2,1)} %get-tuple-element.164, s32[]{:T(128)} %get-tuple-element.163, f32[4,4,128,1024]{3,2,1,0:T(8,128)} %get-tuple-element.153, f32[4,4,128]{2,1,0:T(4,128)S(1)} %get-tuple-element.154, bf16[4,1024,4,128]{3,2,1,0:T(4,128)(2,1)} %bitcast.58), kind=kOutput, calls=%fused_computation.18.clone.1 | convolution fusion | flops 541327360 | bytes 13115904 | tf_op jit(solution)/shard_map/while/body/eval_jaxpr/ghqk,gkhd->gqhd/dot_general | solution.py:55
  174.8 0.1 reshape.141
  174.9 5.7 %gather_fusion = bf16[32,128,4,128]{3,2,1,0:T(4,128)(2,1)} fusion(bf16[8,128,4,128]{3,2,1,0:T(4,128)(2,1)S(1)} %get-tuple-element.177, s32[1024]{0:T(1024)S(1)} %pad_clamp_fusion.2), kind=kCustom, calls=%fused_computation.1.clone.clone.1 | custom fusion | bytes 8388736 | tf_op jit(solution)/shard_map/while/body/eval_jaxpr/gather | solution.py:42
  180.7 3.7 %fusion.43 = f32[4,4,128,1024]{3,2,1,0:T(8,128)S(1)} fusion(bf16[4,1024,4,128]{3,2,1,0:T(4,128)(2,1)} %bitcast.57, bf16[4,4,128,4,128]{2,4,3,1,0:T(8,128)(2,1)} %get-tuple-element.176, s32[]{:T(128)} %get-tuple-element.163), kind=kOutput, calls=%fused_computation.11.clone.1 | convolution fusion | flops 536870912 | bytes 13107712 | tf_op jit(solution)/shard_map/while/body/eval_jaxpr/gqhd,gkhd->ghqk/dot_general | solution.py:45
  184.4 4.7 %fusion.45 = (f32[4,4,128]{2,1,0:T(4,128)S(1)}, f32[4,4,128,1024]{3,2,1,0:T(8,128)}) fusion(f32[4,4,128,1024]{3,2,1,0:T(8,128)S(1)} %fusion.43, pred[4,1024]{1,0:T(4,128)(4,1)S(1)} %broadcast_compare_fusion.2), kind=kOutput, calls=%fused_computation.36.clone.1 | output fusion | flops 12583935 | bytes 16789504 | tf_op jit(solution)/shard_map/while/body/eval_jaxpr/sub | solution.py:52
  189.2 5.8 %gather_fusion.1 = bf16[32,128,4,128]{3,2,1,0:T(4,128)(2,1)} fusion(bf16[8,128,4,128]{3,2,1,0:T(4,128)(2,1)S(1)} %get-tuple-element.174, s32[1024]{0:T(1024)S(1)} %pad_clamp_fusion.2), kind=kCustom, calls=%fused_computation.clone.clone.1 | custom fusion | bytes 8388736 | tf_op jit(solution)/shard_map/while/body/eval_jaxpr/gather | solution.py:43
  194.9 7.3 %fusion.46 = bf16[4,4,128,4,128]{2,4,3,1,0:T(8,128)(2,1)} fusion(bf16[4,4,128,4,128]{2,4,3,1,0:T(8,128)(2,1)} %get-tuple-element.164, s32[]{:T(128)} %get-tuple-element.163, f32[4,4,128,1024]{3,2,1,0:T(8,128)} %get-tuple-element.153, f32[4,4,128]{2,1,0:T(4,128)S(1)} %get-tuple-element.154, bf16[4,1024,4,128]{3,2,1,0:T(4,128)(2,1)} %bitcast.58), kind=kOutput, calls=%fused_computation.18.clone.1 | convolution fusion | flops 541327360 | bytes 13115904 | tf_op jit(solution)/shard_map/while/body/eval_jaxpr/ghqk,gkhd->gqhd/dot_general | solution.py:55
  202.3 5.8 %gather_fusion = bf16[32,128,4,128]{3,2,1,0:T(4,128)(2,1)} fusion(bf16[8,128,4,128]{3,2,1,0:T(4,128)(2,1)S(1)} %get-tuple-element.177, s32[1024]{0:T(1024)S(1)} %pad_clamp_fusion.2), kind=kCustom, calls=%fused_computation.1.clone.clone.1 | custom fusion | bytes 8388736 | tf_op jit(solution)/shard_map/while/body/eval_jaxpr/gather | solution.py:42
  208.1 3.7 %fusion.43 = f32[4,4,128,1024]{3,2,1,0:T(8,128)S(1)} fusion(bf16[4,1024,4,128]{3,2,1,0:T(4,128)(2,1)} %bitcast.57, bf16[4,4,128,4,128]{2,4,3,1,0:T(8,128)(2,1)} %get-tuple-element.176, s32[]{:T(128)} %get-tuple-element.163), kind=kOutput, calls=%fused_computation.11.clone.1 | convolution fusion | flops 536870912 | bytes 13107712 | tf_op jit(solution)/shard_map/while/body/eval_jaxpr/gqhd,gkhd->ghqk/dot_general | solution.py:45
  211.8 4.7 %fusion.45 = (f32[4,4,128]{2,1,0:T(4,128)S(1)}, f32[4,4,128,1024]{3,2,1,0:T(8,128)}) fusion(f32[4,4,128,1024]{3,2,1,0:T(8,128)S(1)} %fusion.43, pred[4,1024]{1,0:T(4,128)(4,1)S(1)} %broadcast_compare_fusion.2), kind=kOutput, calls=%fused_computation.36.clone.1 | output fusion | flops 12583935 | bytes 16789504 | tf_op jit(solution)/shard_map/while/body/eval_jaxpr/sub | solution.py:52
  216.6 5.8 %gather_fusion.1 = bf16[32,128,4,128]{3,2,1,0:T(4,128)(2,1)} fusion(bf16[8,128,4,128]{3,2,1,0:T(4,128)(2,1)S(1)} %get-tuple-element.174, s32[1024]{0:T(1024)S(1)} %pad_clamp_fusion.2), kind=kCustom, calls=%fused_computation.clone.clone.1 | custom fusion | bytes 8388736 | tf_op jit(solution)/shard_map/while/body/eval_jaxpr/gather | solution.py:43
  222.4 7.3 %fusion.46 = bf16[4,4,128,4,128]{2,4,3,1,0:T(8,128)(2,1)} fusion(bf16[4,4,128,4,128]{2,4,3,1,0:T(8,128)(2,1)} %get-tuple-element.164, s32[]{:T(128)} %get-tuple-element.163, f32[4,4,128,1024]{3,2,1,0:T(8,128)} %get-tuple-element.153, f32[4,4,128]{2,1,0:T(4,128)S(1)} %get-tuple-element.154, bf16[4,1024,4,128]{3,2,1,0:T(4,128)(2,1)} %bitcast.58), kind=kOutput, calls=%fused_computation.18.clone.1 | convolution fusion | flops 541327360 | bytes 13115904 | tf_op jit(solution)/shard_map/while/body/eval_jaxpr/ghqk,gkhd->gqhd/dot_general | solution.py:55
  229.8 5.8 %gather_fusion = bf16[32,128,4,128]{3,2,1,0:T(4,128)(2,1)} fusion(bf16[8,128,4,128]{3,2,1,0:T(4,128)(2,1)S(1)} %get-tuple-element.177, s32[1024]{0:T(1024)S(1)} %pad_clamp_fusion.2), kind=kCustom, calls=%fused_computation.1.clone.clone.1 | custom fusion | bytes 8388736 | tf_op jit(solution)/shard_map/while/body/eval_jaxpr/gather | solution.py:42
  235.5 3.6 %fusion.43 = f32[4,4,128,1024]{3,2,1,0:T(8,128)S(1)} fusion(bf16[4,1024,4,128]{3,2,1,0:T(4,128)(2,1)} %bitcast.57, bf16[4,4,128,4,128]{2,4,3,1,0:T(8,128)(2,1)} %get-tuple-element.176, s32[]{:T(128)} %get-tuple-element.163), kind=kOutput, calls=%fused_computation.11.clone.1 | convolution fusion | flops 536870912 | bytes 13107712 | tf_op jit(solution)/shard_map/while/body/eval_jaxpr/gqhd,gkhd->ghqk/dot_general | solution.py:45
  239.3 4.7 %fusion.45 = (f32[4,4,128]{2,1,0:T(4,128)S(1)}, f32[4,4,128,1024]{3,2,1,0:T(8,128)}) fusion(f32[4,4,128,1024]{3,2,1,0:T(8,128)S(1)} %fusion.43, pred[4,1024]{1,0:T(4,128)(4,1)S(1)} %broadcast_compare_fusion.2), kind=kOutput, calls=%fused_computation.36.clone.1 | output fusion | flops 12583935 | bytes 16789504 | tf_op jit(solution)/shard_map/while/body/eval_jaxpr/sub | solution.py:52
  244.0 5.8 %gather_fusion.1 = bf16[32,128,4,128]{3,2,1,0:T(4,128)(2,1)} fusion(bf16[8,128,4,128]{3,2,1,0:T(4,128)(2,1)S(1)} %get-tuple-element.174, s32[1024]{0:T(1024)S(1)} %pad_clamp_fusion.2), kind=kCustom, calls=%fused_computation.clone.clone.1 | custom fusion | bytes 8388736 | tf_op jit(solution)/shard_map/while/body/eval_jaxpr/gather | solution.py:43
  249.8 7.3 %fusion.46 = bf16[4,4,128,4,128]{2,4,3,1,0:T(8,128)(2,1)} fusion(bf16[4,4,128,4,128]{2,4,3,1,0:T(8,128)(2,1)} %get-tuple-element.164, s32[]{:T(128)} %get-tuple-element.163, f32[4,4,128,1024]{3,2,1,0:T(8,128)} %get-tuple-element.153, f32[4,4,128]{2,1,0:T(4,128)S(1)} %get-tuple-element.154, bf16[4,1024,4,128]{3,2,1,0:T(4,128)(2,1)} %bitcast.58), kind=kOutput, calls=%fused_computation.18.clone.1 | convolution fusion | flops 541327360 | bytes 13115904 | tf_op jit(solution)/shard_map/while/body/eval_jaxpr/ghqk,gkhd->gqhd/dot_general | solution.py:55
  257.1 2.9 copy.56
  259.9 51.8 %all_to_all.62 = bf16[16,128,512]{2,1,0:T(8,128)(2,1)S(1)} all-to-all(bf16[16,128,512]{2,1,0:T(8,128)(2,1)S(1)} %copy.56), channel_id=1, replica_groups=mesh['pb'=4,'kv'=8] {'kv'}, dimensions={0} | all-to-all | bytes 4194304 | tf_op jit(solution)/shard_map/all_to_all | solution.py:71
  311.7 1.2 copy.55
  312.9 2.2 copy.58
  (31 shorter events, 0.8 us)
Async XLA Ops:
  6.5 21.8 %all-gather.3.cloned.1.call-start = ((), (), s32[]{:S(2)}) async-start(), calls=%async_computation.4 | async-start | bytes 1310720 | tf_op jit(solution)/shard_map/all_gather | solution.py:27
  30.6 31.7 %all-to-all-start = ((bf16[128,8,512]{0,2,1:T(8,128)(2,1)}), bf16[128,8,512]{0,2,1:T(8,128)(2,1)S(1)}, u32[]{:S(2)}, u32[]{:S(2)}) async-start(bf16[128,8,512]{0,2,1:T(8,128)(2,1)} %bitcast.1), calls=%async_computation | async-start | bytes 2097152 | tf_op jit(solution)/shard_map/all_to_all | solution.py:31
  36.1 19.6 %all-gather.5.cloned.1.call-start = ((), (), s32[]{:S(2)}) async-start(), calls=%async_computation.5 | async-start | bytes 1310720 | tf_op jit(solution)/shard_map/all_gather | solution.py:26
  62.3 29.6 %all-to-all-start.2 = ((bf16[128,8,512]{0,2,1:T(8,128)(2,1)}), bf16[128,8,512]{0,2,1:T(8,128)(2,1)S(1)}, u32[]{:S(2)}, u32[]{:S(2)}) async-start(bf16[128,8,512]{0,2,1:T(8,128)(2,1)} %bitcast.9), calls=%async_computation.2 | async-start | bytes 2097152 | tf_op jit(solution)/shard_map/all_to_all | solution.py:30
  65.9 30.3 %copy-start = (s32[16,8]{0,1:T(8,128)S(1)}, s32[16,8]{0,1:T(8,128)}, u32[]{:S(2)}) copy-start(s32[16,8]{0,1:T(8,128)} %param.10) | copy-start | bytes 1540
  66.0 30.4 %copy-start.1 = (s32[16]{0:T(128)S(1)}, s32[16]{0:T(128)}, u32[]{:S(2)}) copy-start(s32[16]{0:T(128)} %param.11) | copy-start | bytes 196
  91.9 52.2 %all-to-all-start.1 = ((bf16[2,128,4096]{1,0,2:T(2,128)(2,1)}), bf16[2,128,4096]{1,0,2:T(2,128)(2,1)}, u32[]{:S(2)}, u32[]{:S(2)}) async-start(bf16[2,128,4096]{1,0,2:T(2,128)(2,1)} %copy.47), calls=%async_computation.1 | async-start | bytes 4194304 | tf_op jit(solution)/shard_map/all_to_all | solution.py:61
Sparse Core Ops, SparseCore 0:
  8.9 19.4 all-gather.2
  38.5 17.1 all-gather.4
where the time goes:
time: 323 us; the launch traced here: 322 us
  waiting for transfers between devices  107 us (33%)
  local copies, waits for them, and re-layouts  72.7 us (23%)
  blocking collectives  51.8 us (16%)
  matrix products  43.8 us (14%)
  other arithmetic  19.4 us (6%)
  starting transfers between devices  13.5 us (4%)
  between operations  13.5 us (4%)
    all_to_all x1, blocking collectives, per_device(): lax.all_to_all(joined, 'kv', split_axis=0, concat_axis=2, tiled=True)  51.8 us
    all_to_all x1, waiting for transfers between devices, per_device(): lax.all_to_all(query_blocks, 'kv', split_axis=2, concat_axis=0, tiled=True)  41.8 us
    dot_general x4, matrix products, padded_group(): jnp.einsum('ghqk,gkhd->gqhd', weights, listed_values, preferred_element_t...  29.2 us
    gather x4, local copies, waits for them, and re-layouts, padded_group(): value_blocks[group_lists].reshape(members, MOST * BLK, head_local, HD)  23 us
    gather x4, local copies, waits for them, and re-layouts, padded_group(): key_blocks[group_lists].reshape(members, MOST * BLK, head_local, HD)  23 us
    all_gather x1, waiting for transfers between devices, per_device(): lax.all_gather(values, 'pb', axis=0, tiled=True)  21.1 us
    all_to_all x1, waiting for transfers between devices, per_device(): lax.all_to_all(key_whole, 'kv', split_axis=1, concat_axis=0, tiled=True)  19.7 us
    sub x4, other arithmetic, padded_group(): raised = jnp.where(usable, jnp.exp(scores - largest), 0.0)  19 us
  transfers between devices with their start and end apart: 5, of which 5 were waited for; matrix products, arithmetic and copies ran while one was open for 4% of the time, Pallas kernels for 0%

commit v1 on v0

--- a/solution.py
+++ b/solution.py
@@ -1,14 +1,331 @@
+import functools
 import math
 
 import jax
 import jax.numpy as jnp
+import numpy as np
 from jax import lax
+from jax.experimental import pallas as pl
+from jax.experimental.pallas import tpu as pltpu
 from jax.sharding import PartitionSpec as P
 
 HEADS = 32
 HD = 128
 BLK = 128
 MOST = 8
+
+NX, NY, NZ = 2, 2, 4
+CHIPS = NX * NY * NZ
+HALF = HEADS // 2 * HD
+CLASSES = 4
+ROUNDS = HEADS // 2 // CLASSES
+ROUND_COLS = CLASSES * HD
+MESH = pl.DeviceIdType.MESH
+FACTOR = HD ** (-0.5) * math.log2(math.e)
+
+
+def gather_kernel(
+    rows_each, q_rows, q_ref, k_ref, v_ref, bias_ref, out_ref,
+    kv_buf, q_buf, bias_buf, o_buf,
+    recv_sem, send_sem, load_sem, swap_send, swap_recv, out_sem, out_send, out_recv,
+):
+    pb, kv = lax.axis_index("pb"), lax.axis_index("kv")
+    y, core = pb // 2, pb % 2
+    z, x = kv // 2, kv % 2
+    other = 1 - core
+    sibling = (y * 2 + other, kv)
+    x_next = (pb, z * 2 + (1 - x))
+    y_next = ((1 - y) * 2 + core, kv)
+    z_up = (pb, kv + 2)
+    z_down = (pb, kv - 2)
+    has_up, has_down = z < NZ - 1, z > 0
+
+    barrier = pltpu.get_barrier_semaphore()
+
+    def greet(device):
+        pl.semaphore_signal(barrier, inc=1, device_id=device, device_id_type=MESH)
+
+    greet(sibling)
+    greet(x_next)
+    greet(y_next)
+
+    @pl.when(has_up)
+    def _():
+        greet(z_up)
+
+    @pl.when(has_down)
+    def _():
+        greet(z_down)
+
+    def slot_at(cx, cy, cz):
+        return (cy * NZ + cz) * NX + cx
+
+    own = slot_at(x, y, z)
+    mine = pl.ds(pl.multiple_of(core * HALF, HALF), HALF)
+    theirs = pl.ds(pl.multiple_of(other * HALF, HALF), HALF)
+    tokens = pl.ds(pl.multiple_of(core * rows_each, rows_each), rows_each)
+    q_mine = pl.ds(pl.multiple_of(core * q_rows, q_rows), q_rows)
+    q_theirs = pl.ds(pl.multiple_of(other * q_rows, q_rows), q_rows)
+    pairs = [
+        (k_ref, kv_buf.at[own, 0, tokens, :]),
+        (v_ref, kv_buf.at[own, 1, tokens, :]),
+        (q_ref, q_buf.at[q_mine, :]),
+    ]
+    locals_ = [
+        pltpu.make_async_copy(source.at[:, mine], target, load_sem.at[i])
+        for i, (source, target) in enumerate(pairs)
+    ]
+    locals_.append(pltpu.make_async_copy(bias_ref, bias_buf.at[core], load_sem.at[3]))
+    for copy in locals_:
+        copy.start()
+
+    pl.semaphore_wait(barrier, 3 + has_up.astype(jnp.int32) + has_down.astype(jnp.int32))
+
+    def swap(source, target, i):
+        return pltpu.make_async_remote_copy(
+            src_ref=source, dst_ref=target, send_sem=swap_send.at[i], recv_sem=swap_recv.at[i],
+            device_id=sibling, device_id_type=MESH,
+        )
+
+    swaps = [swap(source.at[:, theirs], target, i) for i, (source, target) in enumerate(pairs)]
+    swaps.append(swap(bias_ref, bias_buf.at[core], 3))
+    for copy in swaps:
+        copy.start()
+    for i in range(2):
+        locals_[i].wait()
+        swaps[i].wait_recv()
+
+    kinds = [("z", "x"), ("z", "y"), ("a", "x"), ("a", "y")]
+
+    def columns(r, cl):
+        return pl.ds(pl.multiple_of(r * ROUND_COLS + cl * HD, HD), HD)
+
+    def place(cl, a, b, cz):
+        a_axis = kinds[cl][1]
+        dx, dy = (a, b) if a_axis == "x" else (b, a)
+        return slot_at(1 - x if dx else x, 1 - y if dy else y, cz)
+
+    def copy_of(r, cl, slot, send_slot, device):
+        part = kv_buf.at[slot, :, :, columns(r, cl)]
+        return pltpu.make_async_remote_copy(
+            src_ref=part, dst_ref=part, send_sem=send_sem.at[cl, send_slot],
+            recv_sem=recv_sem.at[r, cl, slot], device_id=device, device_id_type=MESH,
+        )
+
+    def events(cl, mode, r):
+        first, a_axis = kinds[cl]
+        a_next, b_next = (x_next, y_next) if a_axis == "x" else (y_next, x_next)
+
+        def send(slot, send_slot, device):
+            copy = copy_of(r, cl, slot, send_slot, device)
+            if mode == "end":
+                copy.wait_send()
+            else:
+                @pl.when(r > 0)
+                def _():
+                    copy.wait_send()
+
+                copy.start()
+
+        def receive(slot):
+            if mode == "go":
+                copy_of(r, cl, slot, 0, sibling).wait_recv()
+
+        def up(slot, a, cz):
+            @pl.when(has_up)
+            def _():
+                send(slot, a * 5 + cz, z_up)
+
+        def down(slot, a, cz, start=False):
+            @pl.when(has_down)
+            def _():
+                send(slot, a * 5 + (NZ if start else cz), z_down)
+
+        def to_a(slot, cz):
+            send(slot, 10 + cz, a_next)
+
+        def to_b(slot, a, cz):
+            send(slot, 14 + a * NZ + cz, b_next)
+
+        found = []
+
+        def begin():
+            up(own, 0, z)
+            down(own, 0, z, True)
+            to_a(own, z)
+            to_b(own, 0, z)
+
+        found.append((0, begin))
+
+        def along(d, a, upward):
+            def event():
+                cz = z - d if upward else z + d
+
+                @pl.when(cz >= 0 if upward else cz < NZ)
+                def _():
+                    slot = place(cl, a, 0, cz)
+                    receive(slot)
+                    if d < NZ - 1:
+                        (up if upward else down)(slot, a, cz)
+                    if first == "z":
+                        to_a(slot, cz)
+                    to_b(slot, a, cz)
+            return event
+
+        def from_a(d, sign):
+            def event():
+                cz = z + sign * d
+
+                def take():
+                    slot = place(cl, 1, 0, cz)
+                    receive(slot)
+                    if first == "a":
+                        up(slot, 1, cz)
+                        down(slot, 1, cz, True)
+                    to_b(slot, 1, cz)
+
+                if d == 0:
+                    take()
+                else:
+                    pl.when(cz >= 0 if sign < 0 else cz < NZ)(take)
+            return event
+
+        found.append((1, from_a(0, 1)))
+        for d in range(1, NZ):
+            for upward in (True, False):
+                found.append((d, along(d, 0, upward)))
+            if first == "a":
+                for upward in (True, False):
+                    found.append((d + 1, along(d, 1, upward)))
+            else:
+                for sign in (-1, 1):
+                    found.append((d + 1, from_a(d, sign)))
+        return found
+
+    def run_depth(depth, mode, r):
+        for cl in (2, 3, 0, 1):
+            for at, event in events(cl, mode, r):
+                if at == depth:
+                    event()
+
+    def leaves(cl, r):
+        for a in range(2):
+            for cz in range(NZ):
+                copy_of(r, cl, place(cl, a, 1, cz), 0, sibling).wait_recv()
+
+    def attend(cl, r):
+        cols = columns(r, cl)
+        head_keys = kv_buf[:, 0, :, cols].reshape(CHIPS * 2 * rows_each, HD)
+        head_values = kv_buf[:, 1, :, cols].reshape(CHIPS * 2 * rows_each, HD)
+        widened = jnp.concatenate([head_values, jnp.ones_like(head_values)], axis=1)
+        for block in range(2 * q_rows // BLK):
+            rows = pl.ds(block * BLK, BLK)
+            scores = lax.dot_general(
+                q_buf[rows, cols], head_keys, (((1,), (1,)), ((), ())),
+                preferred_element_type=jnp.float32,
+            )
+            per = q_rows // BLK
+            scores = scores * FACTOR + bias_buf[block // per, block % per, 0:1, :]
+            raised = jnp.exp2(scores - jnp.max(scores, axis=1, keepdims=True)).astype(jnp.bfloat16)
+            both = jnp.dot(raised, widened, preferred_element_type=jnp.float32)
+            o_buf[rows, cols] = (both[:, :HD] / both[:, HD:]).astype(jnp.bfloat16)
+
+    def out_copies(r):
+        cols = pl.ds(pl.multiple_of(r * ROUND_COLS, ROUND_COLS), ROUND_COLS)
+        target = out_ref.at[:, pl.ds(pl.multiple_of(core * HALF + r * ROUND_COLS, ROUND_COLS), ROUND_COLS)]
+        keep = pltpu.make_async_copy(o_buf.at[q_mine, cols], target, out_sem.at[r])
+        give = pltpu.make_async_remote_copy(
+            src_ref=o_buf.at[q_theirs, cols], dst_ref=target, send_sem=out_send.at[r],
+            recv_sem=out_recv.at[r], device_id=sibling, device_id_type=MESH,
+        )
+        return keep, give
+
+    def round_body(r, carry):
+        @pl.when(r < ROUNDS)
+        def _():
+            run_depth(0, "go", r)
+
+        @pl.when(r == 0)
+        def _():
+            for i in (2, 3):
+                locals_[i].wait()
+                swaps[i].wait_recv()
+
+        for step in range(CLASSES):
+            @pl.when(r > 0)
+            def _():
+                leaves(step, r - 1)
+                attend(step, r - 1)
+
+            @pl.when(r < ROUNDS)
+            def _():
+                run_depth(step + 1, "go", r)
+
+        @pl.when(r > 0)
+        def _():
+            for copy in out_copies(r - 1):
+                copy.start()
+
+        return carry
+
+    lax.fori_loop(0, ROUNDS + 1, round_body, 0)
+
+    for depth in range(NZ + 1):
+        run_depth(depth, "end", ROUNDS - 1)
+    for copy in swaps:
+        copy.wait_send()
+
+    def finish(r, carry):
+        keep, give = out_copies(r)
+        keep.wait()
+        give.wait()
+        return carry
+
+    lax.fori_loop(0, ROUNDS, finish, 0)
+
+
+def gathered(queries, keys, values, key_lists, counts):
+    q_rows, rows_each = queries.shape[0], keys.shape[0]
+    per = q_rows // BLK
+    key_total = CHIPS * 2 * rows_each
+    position = np.arange(key_total)
+    slot, core = position // (2 * rows_each), position // rows_each % 2
+    slot_x, slot_z, slot_y = slot % NX, slot // NX % NZ, slot // (NX * NZ)
+    device = (slot_y * 2 + core) * (NZ * NX) + slot_z * NX + slot_x
+    block_of = jnp.asarray(device * rows_each // BLK, jnp.int32)
+    start = lax.axis_index("kv") * per
+    lists = lax.dynamic_slice_in_dim(key_lists, start, per, 0)
+    used = lax.dynamic_slice_in_dim(counts, start, per, 0)
+    named = jnp.arange(MOST, dtype=jnp.int32)[None, :] < used[:, None]
+    hit = jnp.any((lists[:, :, None] == block_of[None, None, :]) & named[:, :, None], axis=1)
+    bias = jnp.where(hit, 0.0, -1e30).astype(jnp.float32)
+    bias = jnp.broadcast_to(bias[:, None, :], (per, 8, key_total))
+    anywhere = pl.BlockSpec(memory_space=pl.ANY)
+    flops = 4 * 2 * q_rows * key_total * HALF
+    return pl.pallas_call(
+        functools.partial(gather_kernel, rows_each, q_rows),
+        out_shape=jax.ShapeDtypeStruct(queries.shape, jnp.bfloat16),
+        in_specs=[anywhere] * 4,
+        out_specs=anywhere,
+        scratch_shapes=[
+            pltpu.VMEM((CHIPS, 2, 2 * rows_each, HALF), jnp.bfloat16),
+            pltpu.VMEM((2 * q_rows, HALF), jnp.bfloat16),
+            pltpu.VMEM((2, per, 8, key_total), jnp.float32),
+            pltpu.VMEM((2 * q_rows, HALF), jnp.bfloat16),
+            pltpu.SemaphoreType.DMA((ROUNDS, CLASSES, CHIPS)),
+            pltpu.SemaphoreType.DMA((CLASSES, 22)),
+            pltpu.SemaphoreType.DMA((4,)),
+            pltpu.SemaphoreType.DMA((4,)),
+            pltpu.SemaphoreType.DMA((4,)),
+            pltpu.SemaphoreType.DMA((ROUNDS,)),
+            pltpu.SemaphoreType.DMA((ROUNDS,)),
+            pltpu.SemaphoreType.DMA((ROUNDS,)),
+        ],
+        compiler_params=pltpu.CompilerParams(
+            collective_id=0, has_side_effects=True, vmem_limit_bytes=48 * 1024 * 1024
+        ),
+        cost_estimate=pl.CostEstimate(flops=flops, bytes_accessed=2 * queries.size * 2, transcendentals=0),
+    )(queries, keys, values, bias)
 
 
 def regroup(split_array, kv_count, pb_count):
@@ -73,8 +390,15 @@
 
 
 def solution(mesh):
+    fits = mesh.shape["pb"] == NY * 2 and mesh.shape["kv"] == NX * NZ
+
+    def choose(queries, keys, values, key_lists, counts):
+        small = keys.shape[0] == 32 and queries.shape[0] % BLK == 0
+        work = gathered if fits and small else per_device
+        return work(queries, keys, values, key_lists, counts)
+
     return jax.shard_map(
-        per_device,
+        choose,
         mesh=mesh,
         in_specs=(
             P(("pb", "kv"), None),

time: 323 us -> 89.9 us (0.28)
  waiting for transfers between devices: 107 us -> 0 us
  Pallas kernels: 0 us -> 83 us
  local copies, waits for them, and re-layouts: 72.7 us -> 5.71 us
  blocking collectives: 51.8 us -> 0 us
  matrix products: 43.8 us -> 0 us
  other arithmetic: 19.4 us -> 0.87 us
  starting transfers between devices: 13.5 us -> 0 us
  between operations: 13.5 us -> 0.04 us
    pallas_call x0 -> x1, Pallas kernels: none -> 83 us  [gathered(): pl.pallas_call(functools.partial(gather_kernel, rows_each, q_rows), out_s...]
    all_to_all x3 -> x0, waiting for transfers between devices: 65.8 us -> none  [the longest x1 41.8 us: per_device(): lax.all_to_all(query_blocks, 'kv', split_axis=2, concat_axis=0, tiled=True)]
    all_to_all x1 -> x0, blocking collectives: 51.8 us -> none  [per_device(): lax.all_to_all(joined, 'kv', split_axis=0, concat_axis=2, tiled=True)]
    gather x8 -> x0, local copies, waits for them, and re-layouts: 46 us -> none  [the longest x4 23 us: padded_group(): value_blocks[group_lists].reshape(members, MOST * BLK, head_local, HD)]
    dot_general x8 -> x0, matrix products: 43.8 us -> none  [the longest x4 29.2 us: padded_group(): jnp.einsum('ghqk,gkhd->gqhd', weights, listed_values, preferred_element_t...]
    all_gather x2 -> x0, waiting for transfers between devices: 40 us -> none  [the longest x1 21.1 us: per_device(): lax.all_gather(values, 'pb', axis=0, tiled=True)]
    sub x4 -> x0, other arithmetic: 19 us -> none  [padded_group(): raised = jnp.where(usable, jnp.exp(scores - largest), 0.0)]
    all_to_all x3 -> x0, starting transfers between devices: 13.5 us -> none  [the longest x1 5.51 us: per_device(): lax.all_to_all(value_whole, 'kv', split_axis=1, concat_axis=0, tiled=True)]
  transfers between devices with their start and end apart: 5 -> 0, of which waited for: 5 -> 0; matrix products, arithmetic and copies ran while one was open for 4% -> 0% of each run, Pallas kernels for 0% -> 0%
where the time goes in v1:
time: 89.9 us; the launch traced here: 89.6 us
  Pallas kernels  83 us (92%)
  local copies, waits for them, and re-layouts  5.71 us (6%)
    pallas_call x1, Pallas kernels, gathered(): pl.pallas_call(functools.partial(gather_kernel, rows_each, q_rows), out_s...  83 us
    unnamed x9, local copies, waits for them, and re-layouts  4.81 us

profile of v1, /device:TPU:0, one launch (start us, length us, event | category | flops | bytes accessed | tf_op | source)
XLA Modules:
  0.0 89.6 jit_solution(12036599704437973341)
XLA Ops:
  0.0 0.0 copy-start
  0.0 0.7 dynamic_slice.7
  0.7 0.1 iota_compare_fusion
  0.8 0.0 copy-done
  0.8 0.1 constant_dynamic-slice_fusion
  0.9 0.1 copy.8
  1.0 0.8 and_reduce_fusion
  1.8 0.0 copy-start.1
  1.8 1.6 %copy-done.1 = bf16[256,4096]{1,0:T(8,128)(2,1)S(1)} copy-done((bf16[256,4096]{1,0:T(8,128)(2,1)S(1)}, bf16[256,4096]{1,0:T(8,128)(2,1)}, u32[]{:S(2)}) %copy-start.1) | copy-done | bytes 2097176
  3.4 0.0 copy-start.2
  3.4 0.9 %copy-done.2 = bf16[32,4096]{1,0:T(8,128)(2,1)S(1)} copy-done((bf16[32,4096]{1,0:T(8,128)(2,1)S(1)}, bf16[32,4096]{1,0:T(8,128)(2,1)}, u32[]{:S(2)}) %copy-start.2) | copy-done | bytes 262168
  4.3 0.0 copy-start.3
  4.3 0.9 %copy-done.3 = bf16[32,4096]{1,0:T(8,128)(2,1)S(1)} copy-done((bf16[32,4096]{1,0:T(8,128)(2,1)S(1)}, bf16[32,4096]{1,0:T(8,128)(2,1)}, u32[]{:S(2)}) %copy-start.3) | copy-done | bytes 262168
  5.3 83.0 %shard_map.64 = bf16[256,4096]{1,0:T(8,128)(2,1)S(1)} custom-call(bf16[256,4096]{1,0:T(8,128)(2,1)S(1)} %copy-done.1, bf16[32,4096]{1,0:T(8,128)(2,1)S(1)} %copy-done.2, bf16[32,4096]{1,0:T(8,128)(2,1)S(1)} %copy-done.3, f32[2,8,1024]{2,1,0:T(8,128)S(1)} %broadcast_in_dim.12.bias_ref), custom_call_target="tpu_custom_call" | custom-call | flops 4294967296 | bytes 4194304 | tf_op jit(solution)/shard_map/pallas_call | solution.py:305
  88.3 1.3 %copy.10 = bf16[256,4096]{1,0:T(8,128)(2,1)} copy(bf16[256,4096]{1,0:T(8,128)(2,1)S(1)} %shard_map.64) | data formatting | bytes 4194304
  (2 shorter events, 0.0 us)
Async XLA Ops:
  0.0 0.8 copy-start
  1.8 1.6 %copy-start.1 = (bf16[256,4096]{1,0:T(8,128)(2,1)S(1)}, bf16[256,4096]{1,0:T(8,128)(2,1)}, u32[]{:S(2)}) copy-start(bf16[256,4096]{1,0:T(8,128)(2,1)} %q_ref.1) | copy-start | bytes 6291460
  3.4 0.9 %copy-start.2 = (bf16[32,4096]{1,0:T(8,128)(2,1)S(1)}, bf16[32,4096]{1,0:T(8,128)(2,1)}, u32[]{:S(2)}) copy-start(bf16[32,4096]{1,0:T(8,128)(2,1)} %k_ref.1) | copy-start | bytes 786436
  4.3 0.9 %copy-start.3 = (bf16[32,4096]{1,0:T(8,128)(2,1)S(1)}, bf16[32,4096]{1,0:T(8,128)(2,1)}, u32[]{:S(2)}) copy-start(bf16[32,4096]{1,0:T(8,128)(2,1)} %v_ref.1) | copy-start | bytes 786436

commit v2 on v1

--- a/solution.py
+++ b/solution.py
@@ -3,7 +3,6 @@
 
 import jax
 import jax.numpy as jnp
-import numpy as np
 from jax import lax
 from jax.experimental import pallas as pl
 from jax.experimental.pallas import tpu as pltpu
@@ -24,9 +23,14 @@
 FACTOR = HD ** (-0.5) * math.log2(math.e)
 
 
+def key_block(slot, core, rows_each):
+    cx, cz, cy = slot % NX, slot // NX % NZ, slot // (NX * NZ)
+    return ((cy * 2 + core) * (NZ * NX) + cz * NX + cx) * rows_each // BLK
+
+
 def gather_kernel(
     rows_each, q_rows, q_ref, k_ref, v_ref, bias_ref, out_ref,
-    kv_buf, q_buf, bias_buf, o_buf,
+    kv_buf, q_buf, bias_buf, extra_buf, o_buf,
     recv_sem, send_sem, load_sem, swap_send, swap_recv, out_sem, out_send, out_recv,
 ):
     pb, kv = lax.axis_index("pb"), lax.axis_index("kv")
@@ -89,8 +93,8 @@
 
     swaps = [swap(source.at[:, theirs], target, i) for i, (source, target) in enumerate(pairs)]
     swaps.append(swap(bias_ref, bias_buf.at[core], 3))
-    for copy in swaps:
-        copy.start()
+    for i in (0, 1, 3):
+        swaps[i].start()
     for i in range(2):
         locals_[i].wait()
         swaps[i].wait_recv()
@@ -202,33 +206,42 @@
                     found.append((d + 1, from_a(d, sign)))
         return found
 
-    def run_depth(depth, mode, r):
-        for cl in (2, 3, 0, 1):
-            for at, event in events(cl, mode, r):
-                if at == depth:
-                    event()
+    order = [(depth, cl) for depth in range(NZ + 1) for cl in (2, 3, 0, 1)]
+
+    def run_group(index, mode, r):
+        depth, cl = order[index]
+        for at, event in events(cl, mode, r):
+            if at == depth:
+                event()
+
+    def begin_round(r):
+        for index in range(CLASSES):
+            run_group(index, "go", r)
 
     def leaves(cl, r):
         for a in range(2):
             for cz in range(NZ):
                 copy_of(r, cl, place(cl, a, 1, cz), 0, sibling).wait_recv()
 
-    def attend(cl, r):
+    def attend(cl, r, blocks):
         cols = columns(r, cl)
-        head_keys = kv_buf[:, 0, :, cols].reshape(CHIPS * 2 * rows_each, HD)
-        head_values = kv_buf[:, 1, :, cols].reshape(CHIPS * 2 * rows_each, HD)
-        widened = jnp.concatenate([head_values, jnp.ones_like(head_values)], axis=1)
-        for block in range(2 * q_rows // BLK):
-            rows = pl.ds(block * BLK, BLK)
-            scores = lax.dot_general(
-                q_buf[rows, cols], head_keys, (((1,), (1,)), ((), ())),
-                preferred_element_type=jnp.float32,
-            )
-            per = q_rows // BLK
-            scores = scores * FACTOR + bias_buf[block // per, block % per, 0:1, :]
-            raised = jnp.exp2(scores - jnp.max(scores, axis=1, keepdims=True)).astype(jnp.bfloat16)
-            both = jnp.dot(raised, widened, preferred_element_type=jnp.float32)
-            o_buf[rows, cols] = (both[:, :HD] / both[:, HD:]).astype(jnp.bfloat16)
+        total = CHIPS * 2 * rows_each
+        head_keys = jnp.concatenate([kv_buf[:, 0, :, cols].reshape(total, HD), extra_buf[...]], axis=1)
+        head_values = kv_buf[:, 1, :, cols].reshape(total, HD)
+        head_values = jnp.concatenate([head_values, jnp.ones_like(head_values)], axis=1)
+        lane = lax.broadcasted_iota(jnp.int32, (BLK, HD), 1)
+        scores = []
+        for block in blocks:
+            chosen = jnp.where(lane == block, 1.0, 0.0).astype(jnp.bfloat16)
+            head_queries = jnp.concatenate([q_buf[pl.ds(block * BLK, BLK), cols], chosen], axis=1)
+            scores.append(lax.dot_general(
+                head_queries, head_keys, (((1,), (1,)), ((), ())), preferred_element_type=jnp.float32
+            ))
+        for block, found in zip(blocks, scores):
+            largest = jnp.max(found, axis=1, keepdims=True)
+            raised = jnp.exp2((found - largest) * FACTOR).astype(jnp.bfloat16)
+            both = jnp.dot(raised, head_values, preferred_element_type=jnp.float32)
+            o_buf[pl.ds(block * BLK, BLK), cols] = (both[:, :HD] / both[:, HD:]).astype(jnp.bfloat16)
 
     def out_copies(r):
         cols = pl.ds(pl.multiple_of(r * ROUND_COLS, ROUND_COLS), ROUND_COLS)
@@ -240,26 +253,32 @@
         )
         return keep, give
 
+    blocks_each = 2 * q_rows // BLK // 2
+
     def round_body(r, carry):
         @pl.when(r < ROUNDS)
         def _():
-            run_depth(0, "go", r)
-
-        @pl.when(r == 0)
-        def _():
-            for i in (2, 3):
-                locals_[i].wait()
-                swaps[i].wait_recv()
-
-        for step in range(CLASSES):
+            for index in range(CLASSES, 2 * CLASSES):
+                run_group(index, "go", r)
+
+        for step in range(2 * CLASSES):
+            cl, part = step // 2, step % 2
+
             @pl.when(r > 0)
             def _():
-                leaves(step, r - 1)
-                attend(step, r - 1)
+                if part == 0:
+                    leaves(cl, r - 1)
+                attend(cl, r - 1, range(part * blocks_each, (part + 1) * blocks_each))
 
             @pl.when(r < ROUNDS)
             def _():
-                run_depth(step + 1, "go", r)
+                for index in range(2 * CLASSES + step * 3 // 2, 2 * CLASSES + (step + 1) * 3 // 2):
+                    run_group(index, "go", r)
+
+            if step == CLASSES:
+                @pl.when(r < ROUNDS - 1)
+                def _():
+                    begin_round(r + 1)
 
         @pl.when(r > 0)
         def _():
@@ -268,10 +287,24 @@
 
         return carry
 
+    begin_round(0)
+    swaps[2].start()
+    for i in (2, 3):
+        locals_[i].wait()
+        swaps[i].wait_recv()
+    marks = bias_buf[0] + bias_buf[1]
+    for slot in range(CHIPS):
+        for side in range(2):
+            block = key_block(slot, side, rows_each)
+            start = (slot * 2 + side) * rows_each
+            extra_buf[pl.ds(start, rows_each), :] = jnp.broadcast_to(
+                marks[block:block + 1, :], (rows_each, HD)
+            ).astype(jnp.bfloat16)
+
     lax.fori_loop(0, ROUNDS + 1, round_body, 0)
 
-    for depth in range(NZ + 1):
-        run_depth(depth, "end", ROUNDS - 1)
+    for index in range(len(order)):
+        run_group(index, "end", ROUNDS - 1)
     for copy in swaps:
         copy.wait_send()
 
@@ -288,18 +321,15 @@
     q_rows, rows_each = queries.shape[0], keys.shape[0]
     per = q_rows // BLK
     key_total = CHIPS * 2 * rows_each
-    position = np.arange(key_total)
-    slot, core = position // (2 * rows_each), position // rows_each % 2
-    slot_x, slot_z, slot_y = slot % NX, slot // NX % NZ, slot // (NX * NZ)
-    device = (slot_y * 2 + core) * (NZ * NX) + slot_z * NX + slot_x
-    block_of = jnp.asarray(device * rows_each // BLK, jnp.int32)
-    start = lax.axis_index("kv") * per
-    lists = lax.dynamic_slice_in_dim(key_lists, start, per, 0)
-    used = lax.dynamic_slice_in_dim(counts, start, per, 0)
-    named = jnp.arange(MOST, dtype=jnp.int32)[None, :] < used[:, None]
-    hit = jnp.any((lists[:, :, None] == block_of[None, None, :]) & named[:, :, None], axis=1)
-    bias = jnp.where(hit, 0.0, -1e30).astype(jnp.float32)
-    bias = jnp.broadcast_to(bias[:, None, :], (per, 8, key_total))
+    first = lax.axis_index("pb") % 2 * per
+    lane = jnp.arange(HD, dtype=jnp.int32)
+    row_of_lane = lax.axis_index("kv") * per + lane - first
+    valid = (lane >= first) & (lane < first + per)
+    block = jnp.arange(key_total // BLK, dtype=jnp.int32)[:, None, None, None]
+    same_row = jnp.arange(key_lists.shape[0], dtype=jnp.int32)[None, None, :, None] == row_of_lane[None, :, None, None]
+    named = jnp.arange(MOST, dtype=jnp.int32)[None, :] < counts[:, None]
+    hit = jnp.any((key_lists[None, None] == block) & named[None, None] & same_row, axis=(2, 3))
+    bias = jnp.where(valid[None, :] & ~hit, -1e30, 0.0).astype(jnp.float32)
     anywhere = pl.BlockSpec(memory_space=pl.ANY)
     flops = 4 * 2 * q_rows * key_total * HALF
     return pl.pallas_call(
@@ -310,7 +340,8 @@
         scratch_shapes=[
             pltpu.VMEM((CHIPS, 2, 2 * rows_each, HALF), jnp.bfloat16),
             pltpu.VMEM((2 * q_rows, HALF), jnp.bfloat16),
-            pltpu.VMEM((2, per, 8, key_total), jnp.float32),
+            pltpu.VMEM((2, key_total // BLK, HD), jnp.float32),
+            pltpu.VMEM((key_total, HD), jnp.bfloat16),
             pltpu.VMEM((2 * q_rows, HALF), jnp.bfloat16),
             pltpu.SemaphoreType.DMA((ROUNDS, CLASSES, CHIPS)),
             pltpu.SemaphoreType.DMA((CLASSES, 22)),
@@ -322,7 +353,7 @@
             pltpu.SemaphoreType.DMA((ROUNDS,)),
         ],
         compiler_params=pltpu.CompilerParams(
-            collective_id=0, has_side_effects=True, vmem_limit_bytes=48 * 1024 * 1024
+            collective_id=0, has_side_effects=True, vmem_limit_bytes=61 * 1024 * 1024
         ),
         cost_estimate=pl.CostEstimate(flops=flops, bytes_accessed=2 * queries.size * 2, transcendentals=0),
     )(queries, keys, values, bias)

time: 89.9 us -> 88.4 us (0.983)
  local copies, waits for them, and re-layouts: 5.71 us -> 3.89 us
    unnamed x9 -> x2, local copies, waits for them, and re-layouts: 4.81 us -> 3.89 us
where the time goes in v2:
time: 88.4 us; the launch traced here: 88.2 us
  Pallas kernels  82.7 us (94%)
  local copies, waits for them, and re-layouts  3.89 us (4%)
  other arithmetic  1.59 us (2%)
    pallas_call x1, Pallas kernels, gathered(): pl.pallas_call(functools.partial(gather_kernel, rows_each, q_rows), out_s...  82.7 us
    unnamed x2, local copies, waits for them, and re-layouts  3.89 us

profile of v2, /device:TPU:0, one launch (start us, length us, event | category | flops | bytes accessed | tf_op | source)
XLA Modules:
  0.0 88.2 jit_solution(5607621300718164316)
XLA Ops:
  0.0 0.7 iota_compare_fusion.2
  0.8 0.8 copy.7
  1.5 0.2 and_reduce_fusion
  1.8 0.6 and_select_fusion.bias_ref
  2.4 82.7 %shard_map.55 = bf16[256,4096]{1,0:T(8,128)(2,1)} custom-call(bf16[256,4096]{1,0:T(8,128)(2,1)} %q_ref.1, bf16[32,4096]{1,0:T(8,128)(2,1)} %k_ref.1, bf16[32,4096]{1,0:T(8,128)(2,1)} %v_ref.1, f32[8,128]{1,0:T(8,128)} %and_select_fusion.bias_ref), custom_call_target="tpu_custom_call" | custom-call | flops 4294967296 | bytes 4194304 | tf_op jit(solution)/shard_map/pallas_call | solution.py:335
  85.1 3.1 %copy.9 = bf16[256,4096]{1,0:T(8,128)(2,1)} copy(bf16[256,4096]{1,0:T(8,128)(2,1)} %shard_map.55) | data formatting | bytes 4194304
  (4 shorter events, 0.0 us)

commit v3 on v0

--- a/solution.py
+++ b/solution.py
@@ -1,14 +1,376 @@
+import functools
 import math
 
 import jax
 import jax.numpy as jnp
 from jax import lax
+from jax.experimental import pallas as pl
+from jax.experimental.pallas import tpu as pltpu
 from jax.sharding import PartitionSpec as P
 
 HEADS = 32
 HD = 128
 BLK = 128
 MOST = 8
+
+NX, NY, NZ = 2, 2, 4
+CHIPS = NX * NY * NZ
+HALF = HEADS // 2 * HD
+SERVED = HALF // 4
+ROUNDS = SERVED // HD
+MESH = pl.DeviceIdType.MESH
+FACTOR = HD ** (-0.5) * math.log2(math.e)
+
+
+def axis_coords(axis, a, b, cz):
+    return (a, b, cz) if axis == 0 else (b, a, cz)
+
+
+def key_block(axis, slot, quarter, rows_each):
+    cx, cy, cz = axis_coords(axis, quarter // 2, slot // NZ, slot % NZ)
+    return ((cy * 2 + quarter % 2) * (NZ * NX) + cz * NX + cx) * rows_each // BLK
+
+
+def gather_kernel(
+    rows_each, q_rows, q_ref, k_ref, v_ref, bias_ref, out_ref,
+    kv_buf, q_buf, bias_buf, extra_buf, o_buf,
+    recv_sem, send_sem, load_sem, swap_send, swap_recv, out_sem, out_send, out_recv,
+):
+    pb, kv = lax.axis_index("pb"), lax.axis_index("kv")
+    y, core = pb // 2, pb % 2
+    z, x = kv // 2, kv % 2
+    coord = (x, y)
+
+    def device(axis, flip, swap):
+        cx = 1 - x if flip and axis == 0 else x
+        cy = 1 - y if flip and axis == 1 else y
+        return (cy * 2 + (1 - core if swap else core), z * 2 + cx)
+
+    peers = ((0, 1), (1, 0), (1, 1))
+    z_up = (pb, kv + 2)
+    z_down = (pb, kv - 2)
+    has_up, has_down = z < NZ - 1, z > 0
+
+    barrier = pltpu.get_barrier_semaphore()
+
+    def greet(target):
+        pl.semaphore_signal(barrier, inc=1, device_id=target, device_id_type=MESH)
+
+    greet(device(0, 0, 1))
+    for axis in range(2):
+        greet(device(axis, 1, 0))
+        greet(device(axis, 1, 1))
+
+    @pl.when(has_up)
+    def _():
+        greet(z_up)
+
+    @pl.when(has_down)
+    def _():
+        greet(z_down)
+
+    def heads_of(axis, flip, swap):
+        c = 1 - core if swap else core
+        a = 1 - coord[axis] if flip else coord[axis]
+        return pl.ds(pl.multiple_of(c * HALF + axis * (HALF // 2) + a * SERVED, SERVED), SERVED)
+
+    def quarter(axis):
+        return coord[axis] * 2 + core
+
+    def own(axis):
+        return coord[1 - axis] * NZ + z
+
+    def parts(axis, flip, swap):
+        cols = heads_of(axis, flip, swap)
+        mine = quarter(axis)
+        tokens = pl.ds(pl.multiple_of(mine * rows_each, rows_each), rows_each)
+        return [
+            (k_ref.at[:, cols], kv_buf.at[axis, own(axis), 0, tokens, :]),
+            (v_ref.at[:, cols], kv_buf.at[axis, own(axis), 1, tokens, :]),
+            (bias_ref.at[axis], bias_buf.at[axis, mine]),
+            (q_ref.at[:, cols], q_buf.at[axis, mine]),
+        ]
+
+    def load(axis, i):
+        source, target = parts(axis, 0, 0)[i]
+        return pltpu.make_async_copy(source, target, load_sem.at[axis, i])
+
+    def swap_copy(axis, p, i):
+        source, target = parts(axis, *peers[p])[i]
+        return pltpu.make_async_remote_copy(
+            src_ref=source, dst_ref=target, send_sem=swap_send.at[axis, p, i], recv_sem=swap_recv.at[axis, p, i],
+            device_id=device(axis, *peers[p]), device_id_type=MESH,
+        )
+
+    for i in range(4):
+        for axis in range(2):
+            load(axis, i).start()
+
+    pl.semaphore_wait(barrier, 5 + has_up.astype(jnp.int32) + has_down.astype(jnp.int32))
+
+    def start_swaps(kinds):
+        for p in range(3):
+            for i in kinds:
+                for axis in range(2):
+                    swap_copy(axis, p, i).start()
+
+    def wait_swaps(kinds):
+        for i in kinds:
+            for axis in range(2):
+                load(axis, i).wait()
+                for p in range(3):
+                    swap_copy(axis, p, i).wait_recv()
+
+    def copy_of(r, axis, slot, send_slot, target):
+        cols = pl.ds(pl.multiple_of(r * HD, HD), HD)
+        part = kv_buf.at[axis, slot, :, :, cols]
+        return pltpu.make_async_remote_copy(
+            src_ref=part, dst_ref=part, send_sem=send_sem.at[r, axis, send_slot],
+            recv_sem=recv_sem.at[r, axis, slot], device_id=target, device_id_type=MESH,
+        )
+
+    def place(axis, b, cz):
+        return (1 - coord[1 - axis] if b else coord[1 - axis]) * NZ + cz
+
+    class Steps:
+        def __init__(self, r, axis, across_first, ending):
+            self.r, self.axis, self.across_first, self.ending = r, axis, across_first, ending
+
+        def send(self, slot, send_slot, target):
+            copy = copy_of(self.r, self.axis, slot, send_slot, target)
+            if self.ending:
+                copy.wait_send()
+            else:
+                copy.start()
+
+        def receive(self, slot):
+            if not self.ending:
+                copy_of(self.r, self.axis, slot, 0, z_up).wait_recv()
+
+        def up(self, b, cz):
+            @pl.when(has_up)
+            def _():
+                self.send(place(self.axis, b, cz), b * 5 + cz, z_up)
+
+        def down(self, b, cz, start=False):
+            @pl.when(has_down)
+            def _():
+                self.send(place(self.axis, b, cz), b * 5 + (NZ if start else cz), z_down)
+
+        def across(self, cz):
+            self.send(place(self.axis, 0, cz), 10 + cz, device(1 - self.axis, 1, 0))
+
+        def begin(self):
+            if self.across_first:
+                self.across(z)
+            self.up(0, z)
+            self.down(0, z, True)
+            if not self.across_first:
+                self.across(z)
+
+        def crossed(self):
+            self.receive(place(self.axis, 1, z))
+            self.up(1, z)
+            self.down(1, z, True)
+
+        def along(self, d, b):
+            for upward in (True, False):
+                cz = z - d if upward else z + d
+
+                @pl.when(cz >= 0 if upward else cz < NZ)
+                def _():
+                    self.receive(place(self.axis, b, cz))
+                    if d < NZ - 1:
+                        (self.up if upward else self.down)(b, cz)
+                    if not self.across_first:
+                        self.across(cz)
+
+    def first_round(ending):
+        steps = [Steps(0, axis, True, ending) for axis in range(2)]
+        if ending:
+            for step in steps:
+                step.begin()
+        for step in steps:
+            step.crossed()
+        for d in range(1, NZ):
+            for b in range(2):
+                for step in steps:
+                    step.along(d, b)
+
+    def begin_round(r):
+        for axis in range(2):
+            Steps(r, axis, False, False).begin()
+
+    def later_group(index, r):
+        Steps(r, index % 2, False, False).along(1 + index // 2, 0)
+
+    def leaves(axis, r):
+        for cz in range(NZ):
+            copy_of(r, axis, place(axis, 1, cz), 0, z_up).wait_recv()
+
+    def attend(axis, r, pair):
+        cols = pl.ds(pl.multiple_of(r * HD, HD), HD)
+        total = 2 * NZ * 4 * rows_each
+        head_keys = jnp.concatenate([kv_buf[axis, :, 0, :, cols].reshape(total, HD), extra_buf[axis]], axis=1)
+        head_values = kv_buf[axis, :, 1, :, cols].reshape(total, HD)
+        head_values = jnp.concatenate([head_values, jnp.ones_like(head_values)], axis=1)
+        lane = lax.broadcasted_iota(jnp.int32, (BLK, HD), 1)
+        per = q_rows // BLK
+        scores = []
+        for block in range(per):
+            chosen = jnp.where(lane == pair * per + block, 1.0, 0.0).astype(jnp.bfloat16)
+            head_queries = jnp.concatenate([q_buf[axis, pair, pl.ds(block * BLK, BLK), cols], chosen], axis=1)
+            scores.append(lax.dot_general(
+                head_queries, head_keys, (((1,), (1,)), ((), ())), preferred_element_type=jnp.float32
+            ))
+        for block, found in enumerate(scores):
+            largest = jnp.max(found, axis=1, keepdims=True)
+            raised = jnp.exp2((found - largest) * FACTOR).astype(jnp.bfloat16)
+            both = jnp.dot(raised, head_values, preferred_element_type=jnp.float32)
+            o_buf[axis, pair, pl.ds(block * BLK, BLK), cols] = (both[:, :HD] / both[:, HD:]).astype(jnp.bfloat16)
+
+    def out_columns(axis, r):
+        start = core * HALF + axis * (HALF // 2) + coord[axis] * SERVED + r * HD
+        return out_ref.at[:, pl.ds(pl.multiple_of(start, HD), HD)]
+
+    def out_copies(axis, r):
+        cols = pl.ds(pl.multiple_of(r * HD, HD), HD)
+        found = []
+        for p, (flip, swap) in enumerate(peers):
+            a = 1 - coord[axis] if flip else coord[axis]
+            c = 1 - core if swap else core
+            found.append(pltpu.make_async_remote_copy(
+                src_ref=o_buf.at[axis, a * 2 + c, :, cols], dst_ref=out_columns(axis, r),
+                send_sem=out_send.at[r, axis, p], recv_sem=out_recv.at[r, axis, p],
+                device_id=device(axis, flip, swap), device_id_type=MESH,
+            ))
+        return found
+
+    def out_keep(axis, r):
+        cols = pl.ds(pl.multiple_of(r * HD, HD), HD)
+        return pltpu.make_async_copy(
+            o_buf.at[axis, quarter(axis), :, cols], out_columns(axis, r), out_sem.at[r, axis]
+        )
+
+    def round_body(r, carry):
+        @pl.when(r < ROUNDS)
+        def _():
+            later_group(0, r)
+            later_group(1, r)
+
+        for step in range(8):
+            axis, pair = step // 4, step % 4
+
+            if pair == 0:
+                @pl.when(r > 1)
+                def _():
+                    leaves(axis, r - 1)
+
+            attend(axis, r - 1, pair)
+            if pair == 3:
+                for copy in reversed(out_copies(axis, r - 1)):
+                    copy.start()
+                out_keep(axis, r - 1).start()
+
+            if step < 4:
+                @pl.when(r < ROUNDS)
+                def _():
+                    later_group(2 + step, r)
+
+            if step == 4:
+                @pl.when(r < ROUNDS - 1)
+                def _():
+                    begin_round(r + 1)
+
+        return carry
+
+    start_swaps((0, 1, 2))
+    wait_swaps((0, 1))
+    for axis in range(2):
+        Steps(0, axis, True, False).begin()
+    start_swaps((3,))
+    first_round(False)
+    begin_round(1)
+    wait_swaps((2, 3))
+    for axis in range(2):
+        marks = bias_buf[axis, 0] + bias_buf[axis, 1] + bias_buf[axis, 2] + bias_buf[axis, 3]
+        for slot in range(2 * NZ):
+            for part in range(4):
+                block = key_block(axis, slot, part, rows_each)
+                start = (slot * 4 + part) * rows_each
+                extra_buf[axis, pl.ds(start, rows_each), :] = jnp.broadcast_to(
+                    marks[block:block + 1, :], (rows_each, HD)
+                ).astype(jnp.bfloat16)
+
+    lax.fori_loop(1, ROUNDS + 1, round_body, 0)
+
+    first_round(True)
+
+    def end_round(r, carry):
+        for axis in range(2):
+            step = Steps(r, axis, False, True)
+            step.begin()
+            for d in range(1, NZ):
+                step.along(d, 0)
+        return carry
+
+    lax.fori_loop(1, ROUNDS, end_round, 0)
+    for axis in range(2):
+        for p in range(3):
+            for i in range(4):
+                swap_copy(axis, p, i).wait_send()
+
+    def finish(r, carry):
+        for axis in range(2):
+            out_keep(axis, r).wait()
+            for copy in out_copies(axis, r):
+                copy.wait()
+        return carry
+
+    lax.fori_loop(0, ROUNDS, finish, 0)
+
+
+def gathered(queries, keys, values, key_lists, counts):
+    q_rows, rows_each = queries.shape[0], keys.shape[0]
+    per = q_rows // BLK
+    key_total = CHIPS * 2 * rows_each
+    pb, kv = lax.axis_index("pb"), lax.axis_index("kv")
+    first = (jnp.stack([kv % 2, pb // 2]) * 2 + pb % 2)[:, None] * per
+    lane = jnp.arange(HD, dtype=jnp.int32)[None, :]
+    row_of_lane = (kv * per + lane - first)[:, None, :, None, None]
+    valid = (lane >= first) & (lane < first + per)
+    block = jnp.arange(key_total // BLK, dtype=jnp.int32)[None, :, None, None, None]
+    same_row = jnp.arange(key_lists.shape[0], dtype=jnp.int32)[None, None, None, :, None] == row_of_lane
+    named = jnp.arange(MOST, dtype=jnp.int32)[None, :] < counts[:, None]
+    hit = jnp.any((key_lists[None, None, None] == block) & named[None, None, None] & same_row, axis=(3, 4))
+    bias = jnp.where(valid[:, None, :] & ~hit, -1e30, 0.0).astype(jnp.float32)
+    anywhere = pl.BlockSpec(memory_space=pl.ANY)
+    flops = 4 * 2 * q_rows * key_total * HALF
+    return pl.pallas_call(
+        functools.partial(gather_kernel, rows_each, q_rows),
+        out_shape=jax.ShapeDtypeStruct(queries.shape, jnp.bfloat16),
+        in_specs=[anywhere] * 4,
+        out_specs=pl.BlockSpec(memory_space=pltpu.VMEM),
+        scratch_shapes=[
+            pltpu.VMEM((2, 2 * NZ, 2, 4 * rows_each, SERVED), jnp.bfloat16),
+            pltpu.VMEM((2, 4, q_rows, SERVED), jnp.bfloat16),
+            pltpu.VMEM((2, 4, key_total // BLK, HD), jnp.float32),
+            pltpu.VMEM((2, key_total, HD), jnp.bfloat16),
+            pltpu.VMEM((2, 4, q_rows, SERVED), jnp.bfloat16),
+            pltpu.SemaphoreType.DMA((ROUNDS, 2, 2 * NZ)),
+            pltpu.SemaphoreType.DMA((ROUNDS, 2, 14)),
+            pltpu.SemaphoreType.DMA((2, 4)),
+            pltpu.SemaphoreType.DMA((2, 3, 4)),
+            pltpu.SemaphoreType.DMA((2, 3, 4)),
+            pltpu.SemaphoreType.DMA((ROUNDS, 2)),
+            pltpu.SemaphoreType.DMA((ROUNDS, 2, 3)),
+            pltpu.SemaphoreType.DMA((ROUNDS, 2, 3)),
+        ],
+        compiler_params=pltpu.CompilerParams(
+            collective_id=0, has_side_effects=True, vmem_limit_bytes=61 * 1024 * 1024
+        ),
+        cost_estimate=pl.CostEstimate(flops=flops, bytes_accessed=2 * queries.size * 2, transcendentals=0),
+    )(queries, keys, values, bias)
 
 
 def regroup(split_array, kv_count, pb_count):
@@ -73,8 +435,15 @@
 
 
 def solution(mesh):
+    fits = mesh.shape["pb"] == NY * 2 and mesh.shape["kv"] == NX * NZ
+
+    def choose(queries, keys, values, key_lists, counts):
+        small = keys.shape[0] == 32 and queries.shape[0] % BLK == 0
+        work = gathered if fits and small else per_device
+        return work(queries, keys, values, key_lists, counts)
+
     return jax.shard_map(
-        per_device,
+        choose,
         mesh=mesh,
         in_specs=(
             P(("pb", "kv"), None),

time: 323 us -> 88.6 us (0.27)
  waiting for transfers between devices: 107 us -> 0 us
  Pallas kernels: 0 us -> 82.7 us
  local copies, waits for them, and re-layouts: 72.7 us -> 3.89 us
  blocking collectives: 51.8 us -> 0 us
  matrix products: 43.8 us -> 0 us
  other arithmetic: 19.4 us -> 1.82 us
  starting transfers between devices: 13.5 us -> 0 us
  between operations: 13.5 us -> 0.02 us
    pallas_call x0 -> x1, Pallas kernels: none -> 82.7 us  [gathered(): pl.pallas_call(functools.partial(gather_kernel, rows_each, q_rows), out_s...]
    all_to_all x3 -> x0, waiting for transfers between devices: 65.8 us -> none  [the longest x1 41.8 us: per_device(): lax.all_to_all(query_blocks, 'kv', split_axis=2, concat_axis=0, tiled=True)]
    all_to_all x1 -> x0, blocking collectives: 51.8 us -> none  [per_device(): lax.all_to_all(joined, 'kv', split_axis=0, concat_axis=2, tiled=True)]
    gather x8 -> x0, local copies, waits for them, and re-layouts: 46 us -> none  [the longest x4 23 us: padded_group(): value_blocks[group_lists].reshape(members, MOST * BLK, head_local, HD)]
    dot_general x8 -> x0, matrix products: 43.8 us -> none  [the longest x4 29.2 us: padded_group(): jnp.einsum('ghqk,gkhd->gqhd', weights, listed_values, preferred_element_t...]
    all_gather x2 -> x0, waiting for transfers between devices: 40 us -> none  [the longest x1 21.1 us: per_device(): lax.all_gather(values, 'pb', axis=0, tiled=True)]
    sub x4 -> x1, other arithmetic: 19 us -> 0.07 us  [gathered(): row_of_lane = (kv * per + lane - first)[:, None, :, None, None]]
    all_to_all x3 -> x0, starting transfers between devices: 13.5 us -> none  [the longest x1 5.51 us: per_device(): lax.all_to_all(value_whole, 'kv', split_axis=1, concat_axis=0, tiled=True)]
  transfers between devices with their start and end apart: 5 -> 0, of which waited for: 5 -> 0; matrix products, arithmetic and copies ran while one was open for 4% -> 0% of each run, Pallas kernels for 0% -> 0%
where the time goes in v3:
time: 88.6 us; the launch traced here: 88.4 us
  Pallas kernels  82.7 us (93%)
  local copies, waits for them, and re-layouts  3.89 us (4%)
  other arithmetic  1.82 us (2%)
    pallas_call x1, Pallas kernels, gathered(): pl.pallas_call(functools.partial(gather_kernel, rows_each, q_rows), out_s...  82.7 us
    unnamed x2, local copies, waits for them, and re-layouts  3.89 us

profile of v3, /device:TPU:0, one launch (start us, length us, event | category | flops | bytes accessed | tf_op | source)
XLA Modules:
  0.0 88.4 jit_solution(10811854085335769864)
XLA Ops:
  0.0 0.1 broadcast_add_fusion
  0.1 0.1 compare_and_fusion
  0.2 0.1 broadcast_subtract_fusion
  0.2 0.7 iota_compare_fusion.2
  1.0 0.8 copy.7
  1.8 0.2 and_reduce_fusion
  2.0 0.6 and_select_fusion.bias_ref
  2.6 82.7 %shard_map.55 = bf16[256,4096]{1,0:T(8,128)(2,1)} custom-call(bf16[256,4096]{1,0:T(8,128)(2,1)} %q_ref.1, bf16[32,4096]{1,0:T(8,128)(2,1)} %k_ref.1, bf16[32,4096]{1,0:T(8,128)(2,1)} %v_ref.1, f32[2,8,128]{2,1,0:T(8,128)} %and_select_fusion.bias_ref), custom_call_target="tpu_custom_call" | custom-call | flops 4294967296 | bytes 4194304 | tf_op jit(solution)/shard_map/pallas_call | solution.py:349
  85.3 3.1 %copy.9 = bf16[256,4096]{1,0:T(8,128)(2,1)} copy(bf16[256,4096]{1,0:T(8,128)(2,1)} %shard_map.55) | data formatting | bytes 4194304
  (3 shorter events, 0.0 us)

commit v4 on v3

--- a/solution.py
+++ b/solution.py
@@ -32,7 +32,7 @@
 
 
 def gather_kernel(
-    rows_each, q_rows, q_ref, k_ref, v_ref, bias_ref, out_ref,
+    rows_each, q_rows, q_ref, k_ref, v_ref, lists_ref, counts_ref, out_ref,
     kv_buf, q_buf, bias_buf, extra_buf, o_buf,
     recv_sem, send_sem, load_sem, swap_send, swap_recv, out_sem, out_send, out_recv,
 ):
@@ -87,7 +87,7 @@
         return [
             (k_ref.at[:, cols], kv_buf.at[axis, own(axis), 0, tokens, :]),
             (v_ref.at[:, cols], kv_buf.at[axis, own(axis), 1, tokens, :]),
-            (bias_ref.at[axis], bias_buf.at[axis, mine]),
+            (bias_buf.at[axis, mine], bias_buf.at[axis, mine]),
             (q_ref.at[:, cols], q_buf.at[axis, mine]),
         ]
 
@@ -102,9 +102,26 @@
             device_id=device(axis, *peers[p]), device_id_type=MESH,
         )
 
-    for i in range(4):
+    for i in (0, 1, 3):
         for axis in range(2):
             load(axis, i).start()
+
+    per = q_rows // BLK
+    for axis in range(2):
+        tile = bias_buf.shape[2:]
+        block_id = lax.broadcasted_iota(jnp.int32, tile, 0)
+        lane_id = lax.broadcasted_iota(jnp.int32, tile, 1)
+        tally = jnp.zeros(tile, jnp.float32)
+        for one in range(per):
+            row = kv * per + one
+            used = counts_ref[row]
+            hit = jnp.zeros(tile, jnp.float32)
+            for entry in range(MOST):
+                named = jnp.where(entry < used, lists_ref[row, entry], -1)
+                hit = jnp.where(block_id == named, 1.0, hit)
+            wanted = lane_id == quarter(axis) * per + one
+            tally = jnp.where(wanted, jnp.where(hit > 0.5, 0.0, -1e30), tally)
+        bias_buf[axis, quarter(axis)] = tally
 
     pl.semaphore_wait(barrier, 5 + has_up.astype(jnp.int32) + has_down.astype(jnp.int32))
 
@@ -117,7 +134,8 @@
     def wait_swaps(kinds):
         for i in kinds:
             for axis in range(2):
-                load(axis, i).wait()
+                if i != 2:
+                    load(axis, i).wait()
                 for p in range(3):
                     swap_copy(axis, p, i).wait_recv()
 
@@ -208,26 +226,26 @@
         for cz in range(NZ):
             copy_of(r, axis, place(axis, 1, cz), 0, z_up).wait_recv()
 
-    def attend(axis, r, pair):
+    total = 2 * NZ * 4 * rows_each
+
+    def attend(axis, r, half):
         cols = pl.ds(pl.multiple_of(r * HD, HD), HD)
-        total = 2 * NZ * 4 * rows_each
-        head_keys = jnp.concatenate([kv_buf[axis, :, 0, :, cols].reshape(total, HD), extra_buf[axis]], axis=1)
+        if half == 0:
+            extra_buf[axis, 0:HD, :] = jnp.swapaxes(kv_buf[axis, :, 0, :, cols].reshape(total, HD), 0, 1)
+        head_keys = extra_buf[axis]
         head_values = kv_buf[axis, :, 1, :, cols].reshape(total, HD)
         head_values = jnp.concatenate([head_values, jnp.ones_like(head_values)], axis=1)
-        lane = lax.broadcasted_iota(jnp.int32, (BLK, HD), 1)
-        per = q_rows // BLK
-        scores = []
-        for block in range(per):
-            chosen = jnp.where(lane == pair * per + block, 1.0, 0.0).astype(jnp.bfloat16)
-            head_queries = jnp.concatenate([q_buf[axis, pair, pl.ds(block * BLK, BLK), cols], chosen], axis=1)
-            scores.append(lax.dot_general(
-                head_queries, head_keys, (((1,), (1,)), ((), ())), preferred_element_type=jnp.float32
-            ))
-        for block, found in enumerate(scores):
-            largest = jnp.max(found, axis=1, keepdims=True)
-            raised = jnp.exp2((found - largest) * FACTOR).astype(jnp.bfloat16)
-            both = jnp.dot(raised, head_values, preferred_element_type=jnp.float32)
-            o_buf[axis, pair, pl.ds(block * BLK, BLK), cols] = (both[:, :HD] / both[:, HD:]).astype(jnp.bfloat16)
+        rows = 2 * q_rows
+        row_block = lax.broadcasted_iota(jnp.int32, (rows, HD), 0) // BLK + half * (rows // BLK)
+        chosen = (row_block == lax.broadcasted_iota(jnp.int32, (rows, HD), 1)).astype(jnp.float32).astype(jnp.bfloat16)
+        sources = slice(2 * half, 2 * half + 2)
+        head_queries = jnp.concatenate([q_buf[axis, sources, :, cols].reshape(rows, HD), chosen], axis=1)
+        scores = jnp.dot(head_queries, head_keys, preferred_element_type=jnp.float32)
+        largest = jnp.max(scores, axis=1, keepdims=True)
+        raised = jnp.exp2((scores - largest) * FACTOR).astype(jnp.bfloat16)
+        both = jnp.dot(raised, head_values, preferred_element_type=jnp.float32)
+        done = (both[:, :HD] / both[:, HD:]).astype(jnp.bfloat16)
+        o_buf[axis, sources, :, cols] = done.reshape(2, q_rows, HD)
 
     def out_columns(axis, r):
         start = core * HALF + axis * (HALF // 2) + coord[axis] * SERVED + r * HD
@@ -258,26 +276,27 @@
             later_group(0, r)
             later_group(1, r)
 
-        for step in range(8):
-            axis, pair = step // 4, step % 4
-
-            if pair == 0:
+        for step in range(4):
+            axis, half = step // 2, step % 2
+
+            if half == 0:
                 @pl.when(r > 1)
                 def _():
                     leaves(axis, r - 1)
 
-            attend(axis, r - 1, pair)
-            if pair == 3:
+            attend(axis, r - 1, half)
+            if half == 1:
                 for copy in reversed(out_copies(axis, r - 1)):
                     copy.start()
                 out_keep(axis, r - 1).start()
 
-            if step < 4:
+            if step < 2:
                 @pl.when(r < ROUNDS)
                 def _():
-                    later_group(2 + step, r)
-
-            if step == 4:
+                    later_group(2 + 2 * step, r)
+                    later_group(3 + 2 * step, r)
+
+            if step == 2:
                 @pl.when(r < ROUNDS - 1)
                 def _():
                     begin_round(r + 1)
@@ -294,13 +313,12 @@
     wait_swaps((2, 3))
     for axis in range(2):
         marks = bias_buf[axis, 0] + bias_buf[axis, 1] + bias_buf[axis, 2] + bias_buf[axis, 3]
-        for slot in range(2 * NZ):
-            for part in range(4):
-                block = key_block(axis, slot, part, rows_each)
-                start = (slot * 4 + part) * rows_each
-                extra_buf[axis, pl.ds(start, rows_each), :] = jnp.broadcast_to(
-                    marks[block:block + 1, :], (rows_each, HD)
-                ).astype(jnp.bfloat16)
+        spread = jnp.concatenate([
+            jnp.broadcast_to(marks[block:block + 1, :], (rows_each, HD))
+            for slot in range(2 * NZ) for part in range(4)
+            for block in [key_block(axis, slot, part, rows_each)]
+        ], axis=0)
+        extra_buf[axis, HD:2 * HD, :] = jnp.swapaxes(spread, 0, 1).astype(jnp.bfloat16)
 
     lax.fori_loop(1, ROUNDS + 1, round_body, 0)
 
@@ -332,30 +350,20 @@
 
 def gathered(queries, keys, values, key_lists, counts):
     q_rows, rows_each = queries.shape[0], keys.shape[0]
-    per = q_rows // BLK
     key_total = CHIPS * 2 * rows_each
-    pb, kv = lax.axis_index("pb"), lax.axis_index("kv")
-    first = (jnp.stack([kv % 2, pb // 2]) * 2 + pb % 2)[:, None] * per
-    lane = jnp.arange(HD, dtype=jnp.int32)[None, :]
-    row_of_lane = (kv * per + lane - first)[:, None, :, None, None]
-    valid = (lane >= first) & (lane < first + per)
-    block = jnp.arange(key_total // BLK, dtype=jnp.int32)[None, :, None, None, None]
-    same_row = jnp.arange(key_lists.shape[0], dtype=jnp.int32)[None, None, None, :, None] == row_of_lane
-    named = jnp.arange(MOST, dtype=jnp.int32)[None, :] < counts[:, None]
-    hit = jnp.any((key_lists[None, None, None] == block) & named[None, None, None] & same_row, axis=(3, 4))
-    bias = jnp.where(valid[:, None, :] & ~hit, -1e30, 0.0).astype(jnp.float32)
-    anywhere = pl.BlockSpec(memory_space=pl.ANY)
+    far = pl.BlockSpec(memory_space=pltpu.HBM)
+    scalars = pl.BlockSpec(memory_space=pltpu.SMEM)
     flops = 4 * 2 * q_rows * key_total * HALF
     return pl.pallas_call(
         functools.partial(gather_kernel, rows_each, q_rows),
         out_shape=jax.ShapeDtypeStruct(queries.shape, jnp.bfloat16),
-        in_specs=[anywhere] * 4,
-        out_specs=pl.BlockSpec(memory_space=pltpu.VMEM),
+        in_specs=[far] * 3 + [scalars] * 2,
+        out_specs=pl.BlockSpec(memory_space=pl.ANY),
         scratch_shapes=[
             pltpu.VMEM((2, 2 * NZ, 2, 4 * rows_each, SERVED), jnp.bfloat16),
             pltpu.VMEM((2, 4, q_rows, SERVED), jnp.bfloat16),
             pltpu.VMEM((2, 4, key_total // BLK, HD), jnp.float32),
-            pltpu.VMEM((2, key_total, HD), jnp.bfloat16),
+            pltpu.VMEM((2, 2 * HD, key_total), jnp.bfloat16),
             pltpu.VMEM((2, 4, q_rows, SERVED), jnp.bfloat16),
             pltpu.SemaphoreType.DMA((ROUNDS, 2, 2 * NZ)),
             pltpu.SemaphoreType.DMA((ROUNDS, 2, 14)),
@@ -367,10 +375,10 @@
             pltpu.SemaphoreType.DMA((ROUNDS, 2, 3)),
         ],
         compiler_params=pltpu.CompilerParams(
-            collective_id=0, has_side_effects=True, vmem_limit_bytes=61 * 1024 * 1024
+            collective_id=0, has_side_effects=True, vmem_limit_bytes=48 * 1024 * 1024
         ),
         cost_estimate=pl.CostEstimate(flops=flops, bytes_accessed=2 * queries.size * 2, transcendentals=0),
-    )(queries, keys, values, bias)
+    )(queries, keys, values, key_lists, counts)
 
 
 def regroup(split_array, kv_count, pb_count):

time: 88.6 us -> 87.4 us (0.986)
  local copies, waits for them, and re-layouts: 3.89 us -> 6.22 us
  other arithmetic: 1.82 us -> 0 us
  Pallas kernels: 82.7 us -> 80.9 us
    unnamed x2 -> x10, local copies, waits for them, and re-layouts: 3.89 us -> 6.22 us
    pallas_call x1, Pallas kernels: 82.7 us -> 80.9 us  [gathered(): pl.pallas_call(functools.partial(gather_kernel, rows_each, q_rows), out_s...]
where the time goes in v4:
time: 87.4 us; the launch traced here: 87.2 us
  Pallas kernels  80.9 us (93%)
  local copies, waits for them, and re-layouts  6.22 us (7%)
    pallas_call x1, Pallas kernels, gathered(): pl.pallas_call(functools.partial(gather_kernel, rows_each, q_rows), out_s...  80.9 us
    unnamed x10, local copies, waits for them, and re-layouts  6.22 us

profile of v4, /device:TPU:0, one launch (start us, length us, event | category | flops | bytes accessed | tf_op | source)
XLA Modules:
  0.0 87.2 jit_solution(4996655864004238707)
XLA Ops:
  0.0 0.8 copy.6.lists_ref
  0.8 0.0 copy-start
  0.8 1.6 %copy-done = bf16[256,4096]{1,0:T(8,128)(2,1)S(1)} copy-done((bf16[256,4096]{1,0:T(8,128)(2,1)S(1)}, bf16[256,4096]{1,0:T(8,128)(2,1)}, u32[]{:S(2)}) %copy-start) | copy-done | bytes 2097176
  2.3 0.0 copy-start.1
  2.4 0.9 %copy-done.1 = bf16[32,4096]{1,0:T(8,128)(2,1)S(1)} copy-done((bf16[32,4096]{1,0:T(8,128)(2,1)S(1)}, bf16[32,4096]{1,0:T(8,128)(2,1)}, u32[]{:S(2)}) %copy-start.1) | copy-done | bytes 262168
  3.3 0.0 copy-start.2
  3.3 0.9 %copy-done.2 = bf16[32,4096]{1,0:T(8,128)(2,1)S(1)} copy-done((bf16[32,4096]{1,0:T(8,128)(2,1)S(1)}, bf16[32,4096]{1,0:T(8,128)(2,1)}, u32[]{:S(2)}) %copy-start.2) | copy-done | bytes 262168
  4.3 0.0 copy-start.3
  4.3 0.7 copy-done.3
  4.9 80.9 %shard_map.55 = bf16[256,4096]{1,0:T(8,128)(2,1)S(1)} custom-call(bf16[256,4096]{1,0:T(8,128)(2,1)S(1)} %copy-done, bf16[32,4096]{1,0:T(8,128)(2,1)S(1)} %copy-done.1, bf16[32,4096]{1,0:T(8,128)(2,1)S(1)} %copy-done.2, s32[16,8]{1,0:T(8,128)S(1)} %copy.6.lists_ref, s32[16]{0:T(128)S(1)} %copy-done.3), custom_call_target="tpu_custom_call" | custom-call | flops 4294967296 | bytes 4194304 | tf_op jit(solution)/shard_map/pallas_call | solution.py:357
  85.8 1.3 %copy.8 = bf16[256,4096]{1,0:T(8,128)(2,1)} copy(bf16[256,4096]{1,0:T(8,128)(2,1)S(1)} %shard_map.55) | data formatting | bytes 4194304
Async XLA Ops:
  0.8 1.6 %copy-start = (bf16[256,4096]{1,0:T(8,128)(2,1)S(1)}, bf16[256,4096]{1,0:T(8,128)(2,1)}, u32[]{:S(2)}) copy-start(bf16[256,4096]{1,0:T(8,128)(2,1)} %q_ref.1) | copy-start | bytes 6291460
  2.3 0.9 %copy-start.1 = (bf16[32,4096]{1,0:T(8,128)(2,1)S(1)}, bf16[32,4096]{1,0:T(8,128)(2,1)}, u32[]{:S(2)}) copy-start(bf16[32,4096]{1,0:T(8,128)(2,1)} %k_ref.1) | copy-start | bytes 786436
  3.3 0.9 %copy-start.2 = (bf16[32,4096]{1,0:T(8,128)(2,1)S(1)}, bf16[32,4096]{1,0:T(8,128)(2,1)}, u32[]{:S(2)}) copy-start(bf16[32,4096]{1,0:T(8,128)(2,1)} %v_ref.1) | copy-start | bytes 786436
  4.3 0.7 copy-start.3

commit v5 on v4

--- a/solution.py
+++ b/solution.py
@@ -271,6 +271,10 @@
         )
 
     def round_body(r, carry):
+        @pl.when(r < ROUNDS - 1)
+        def _():
+            begin_round(r + 1)
+
         @pl.when(r < ROUNDS)
         def _():
             later_group(0, r)
@@ -296,11 +300,6 @@
                     later_group(2 + 2 * step, r)
                     later_group(3 + 2 * step, r)
 
-            if step == 2:
-                @pl.when(r < ROUNDS - 1)
-                def _():
-                    begin_round(r + 1)
-
         return carry
 
     start_swaps((0, 1, 2))
@@ -308,8 +307,8 @@
     for axis in range(2):
         Steps(0, axis, True, False).begin()
     start_swaps((3,))
+    begin_round(1)
     first_round(False)
-    begin_round(1)
     wait_swaps((2, 3))
     for axis in range(2):
         marks = bias_buf[axis, 0] + bias_buf[axis, 1] + bias_buf[axis, 2] + bias_buf[axis, 3]
@@ -375,7 +374,7 @@
             pltpu.SemaphoreType.DMA((ROUNDS, 2, 3)),
         ],
         compiler_params=pltpu.CompilerParams(
-            collective_id=0, has_side_effects=True, vmem_limit_bytes=48 * 1024 * 1024
+            collective_id=0, has_side_effects=True, vmem_limit_bytes=61 * 1024 * 1024
         ),
         cost_estimate=pl.CostEstimate(flops=flops, bytes_accessed=2 * queries.size * 2, transcendentals=0),
     )(queries, keys, values, key_lists, counts)

time: 87.4 us -> 75.7 us (0.87)
  Pallas kernels: 80.9 us -> 71 us
  local copies, waits for them, and re-layouts: 6.22 us -> 4.48 us
    pallas_call x1, Pallas kernels: 80.9 us -> 71 us  [gathered(): pl.pallas_call(functools.partial(gather_kernel, rows_each, q_rows), out_s...]
    unnamed x10 -> x2, local copies, waits for them, and re-layouts: 6.22 us -> 4.48 us
where the time goes in v5:
time: 75.7 us; the launch traced here: 75.5 us
  Pallas kernels  71 us (94%)
  local copies, waits for them, and re-layouts  4.48 us (6%)
    pallas_call x1, Pallas kernels, gathered(): pl.pallas_call(functools.partial(gather_kernel, rows_each, q_rows), out_s...  71 us
    unnamed x2, local copies, waits for them, and re-layouts  4.48 us

profile of v5, /device:TPU:0, one launch (start us, length us, event | category | flops | bytes accessed | tf_op | source)
XLA Modules:
  0.0 75.5 jit_solution(1756090210047857782)
XLA Ops:
  0.0 1.4 %copy.6.lists_ref = s32[16,8]{1,0:T(8,128)} copy(s32[16,8]{0,1:T(8,128)} %param.8) | data formatting | bytes 1024 | tf_op args[3]
  1.4 71.0 %shard_map.55 = bf16[256,4096]{1,0:T(8,128)(2,1)} custom-call(bf16[256,4096]{1,0:T(8,128)(2,1)} %q_ref.1, bf16[32,4096]{1,0:T(8,128)(2,1)} %k_ref.1, bf16[32,4096]{1,0:T(8,128)(2,1)} %v_ref.1, s32[16,8]{1,0:T(8,128)} %copy.6.lists_ref, s32[16]{0:T(128)} %counts_ref.1), custom_call_target="tpu_custom_call" | custom-call | flops 4294967296 | bytes 4194304 | tf_op jit(solution)/shard_map/pallas_call | solution.py:356
  72.3 3.1 %copy.8 = bf16[256,4096]{1,0:T(8,128)(2,1)} copy(bf16[256,4096]{1,0:T(8,128)(2,1)} %shard_map.55) | data formatting | bytes 4194304
